TPU v7x, 32 devices: a whole 2x2x4 slice. The times are simulated.
32 devices in a mesh: scan: 16 (over z, y, x), mode: 2 (over core).
Axes of the slice: x: 2, y: 2, z: 4, core: 2. Of those that a mesh axis runs over, the one named last changes fastest.
Arguments:
- object_field: float32 [2, 640, 1152], P(None, 'scan'), may hold values from -4.5 to 4.5
- probe: float32 [8, 2, 512, 512], P('mode'), may hold values from -1.5 to 1.5
- amplitude: float32 [16, 512, 512], P('scan'), may hold values from 0.2 to 1.8
- pos_row: int32 [16], P('scan'), may hold values from 0 to 128, as said below
- pos_col: int32 [16], P('scan'), may hold values from 0 to 640, as said below
- strip_of: int32 [16], P('scan'), may hold values from 0 to 15, each once
Outputs:
- object_grad: float32 [2, 640, 1152], P(None, 'scan')
- probe_grad: float32 [8, 2, 512, 512], P('mode')
Inputs may be any that keep to these rules, and one draw needn't show every extreme that they name: Pattern p covers object rows pos_row[p] to pos_row[p] + 511; the smallest and the largest allowed value both occur. Pattern p covers object columns pos_col[p] to pos_col[p] + 511; the smallest and the largest allowed value both occur.
All inputs are finite; a program needn't handle non-finite values.
Results may differ from a plain program's by a relative error of at most 0.0055.
The roundings to bfloat16 on the way count: a program that leaves them out, or rounds other values in their place, can miss the bound.
Values may be sent and summed in bfloat16 or wider, within the bound.
A program may use at most 128 MiB of HBM per device.

v0:
```python
import math
import jax
import jax.numpy as jnp
from jax import lax
from jax.sharding import PartitionSpec as P


def dft_table(sign_factor, probe_size):
    positions = jnp.arange(probe_size, dtype=jnp.int32)
    products = positions[:, None] * positions[None, :] % probe_size
    angle_table = products.astype(jnp.float32) * (2.0 * math.pi / probe_size)
    norm_scale = 1.0 / math.sqrt(probe_size)
    cosine = jnp.cos(angle_table) * norm_scale
    sine_part = jnp.sin(angle_table) * (sign_factor * norm_scale)
    return jnp.stack([jnp.stack([cosine, sine_part]), jnp.stack([-sine_part, cosine])]).astype(
        jnp.bfloat16
    )


def transform(field_wave, matrix_table):
    half_wave = jnp.einsum(
        "oiab,pmibx->pmoax", matrix_table, field_wave, preferred_element_type=jnp.float32
    ).astype(jnp.bfloat16)
    return jnp.einsum(
        "pmiax,oixy->pmoay", half_wave, matrix_table, preferred_element_type=jnp.float32
    )


def shards(object_field, probe, amplitude, pos_row, pos_col, strip_of):
    probe_size = probe.shape[-1]
    strip_rows = object_field.shape[1]
    obj_cols = object_field.shape[2]
    pat_count = pos_row.shape[0]
    devices = lax.axis_size("scan")
    held_rows = devices * strip_rows
    all_strips, all_cols = (
        lax.all_gather(strip_of, "scan", axis=0, tiled=True),
        lax.all_gather(pos_col, "scan", axis=0, tiled=True),
    )
    device_ids = jnp.arange(devices, dtype=jnp.int32)
    owner_of = jnp.sum(
        jnp.where(all_strips[None, :] == device_ids[:, None], device_ids[None, :], 0), axis=1
    )
    inside_rows = jnp.tile(jnp.arange(strip_rows, dtype=jnp.int32), devices)
    held_of_window = jnp.repeat(owner_of, strip_rows) * strip_rows + inside_rows
    window_of_held = jnp.repeat(all_strips, strip_rows) * strip_rows + inside_rows

    def patch_rows(row_start):
        return lax.dynamic_slice_in_dim(held_of_window, row_start, probe_size)

    held_index = jax.vmap(patch_rows)(pos_row)
    object_half = object_field.astype(jnp.bfloat16)
    gathered = lax.all_gather(object_half, "scan", axis=1, tiled=True)

    def take_patch(rows_wanted, col_start):
        band_rows = jnp.take(gathered, rows_wanted, axis=1)
        return lax.dynamic_slice_in_dim(band_rows, col_start, probe_size, 2)

    patches = jax.vmap(take_patch)(held_index, pos_col)
    patch_wide = patches.astype(jnp.float32)
    patch_re = patch_wide[:, None, 0]
    patch_im = patch_wide[:, None, 1]
    probe_re = probe[:, 0]
    probe_im = probe[:, 1]
    exit_re = probe_re * patch_re - probe_im * patch_im
    exit_im = probe_re * patch_im + probe_im * patch_re
    exit_wave = jnp.stack([exit_re, exit_im], axis=2).astype(jnp.bfloat16)
    forward = dft_table(1.0, probe_size)
    inverse = dft_table(-1.0, probe_size)
    far_field = transform(exit_wave, forward)
    local_power = jnp.sum(
        far_field[:, :, 0] * far_field[:, :, 0] + far_field[:, :, 1] * far_field[:, :, 1], axis=1
    )
    intensity = lax.psum(local_power, "mode")
    scale_factor = 1.0 - amplitude / jnp.sqrt(jnp.maximum(intensity, 0.25))
    residual_wave = (far_field * scale_factor[:, None, None]).astype(jnp.bfloat16)
    back_wave = transform(residual_wave, inverse)
    back_re = back_wave[:, :, 0]
    back_im = back_wave[:, :, 1]
    grad_re = jnp.sum(probe_re * back_re + probe_im * back_im, axis=1)
    grad_im = jnp.sum(probe_re * back_im - probe_im * back_re, axis=1)
    patch_grad = jnp.stack([grad_re, grad_im], axis=1)
    term_re = jnp.sum(patch_re * back_re + patch_im * back_im, axis=0)
    term_im = jnp.sum(patch_re * back_im - patch_im * back_re, axis=0)
    probe_grad = lax.psum(jnp.stack([term_re, term_im], axis=1), "scan")
    patch_grad = lax.psum(patch_grad, "mode")

    def band_of(grad_piece, row_start):
        band_rows = jnp.zeros((2, held_rows, probe_size), jnp.float32)
        band_rows = lax.dynamic_update_slice_in_dim(band_rows, grad_piece, row_start, 1)
        return jnp.take(band_rows, window_of_held, axis=1)

    bands = jax.vmap(band_of)(patch_grad, pos_row)
    received = lax.all_to_all(bands, "scan", split_axis=2, concat_axis=0, tiled=True)

    def add_piece(slot_index, strip_total):
        col_start = all_cols[slot_index]
        current = lax.dynamic_slice_in_dim(strip_total, col_start, probe_size, 2)
        return lax.dynamic_update_slice_in_dim(
            strip_total, current + received[slot_index], col_start, 2
        )

    object_grad = lax.fori_loop(
        0, devices * pat_count, add_piece, jnp.zeros((2, strip_rows, obj_cols), jnp.float32)
    )
    return (object_grad, probe_grad)


def solution(mesh):
    return jax.shard_map(
        shards,
        mesh=mesh,
        in_specs=(
            P(None, "scan", None),
            P("mode", None, None, None),
            P("scan", None, None),
            P("scan"),
            P("scan"),
            P("scan"),
        ),
        out_specs=(P(None, "scan", None), P("mode", None, None, None)),
        check_vma=False,
    )
```

profile of v0, /device:TPU:0, one launch (start us, length us, event | category | flops | bytes accessed | tf_op | source)
XLA Modules:
  0.0 562.3 jit_solution(8527928719411964411)
XLA Ops:
  7.2 1.9 copy.127
  11.1 7.8 %fusion.57 = (f32[4,1,512,512]{3,2,1,0:T(8,128)}, f32[4,1,512,512]{3,2,1,0:T(8,128)}) fusion(f32[4,2,512,512]{3,2,1,0:T(8,128)} %param.11), kind=kLoop, calls=%fused_computation.103 | loop fusion | bytes 16777216 | tf_op jit(solution)/shard_map/slice | solution.py:63
  18.9 5.3 copy.123
  24.1 5.3 copy.122
  31.5 16.2 %all-reduce.3 = (s32[16]{0:T(128)S(1)}, s32[16]{0:T(128)S(1)}) all-reduce(s32[16]{0:T(128)S(1)} %dynamic-update-slice.5, s32[16]{0:T(128)S(1)} %dynamic-update-slice.6), channel_id=1, replica_groups=mesh['scan'=16,'mode'=2] {'scan'}, use_global_device_ids=true, to_apply=%add.1 | all-reduce | flops 32 | bytes 256
  48.1 4.0 multiply_convert_fusion.3
  52.1 4.4 multiply_convert_fusion.1
  56.5 4.0 negate_convert_fusion
  60.5 2.2 fusion.43
  62.7 17.7 %all-gather.2.cloned.1.call-done = bf16[2,640,1152]{2,0,1:T(2,128)(2,1)} async-done(((bf16[2,40,1152]{2,0,1:T(2,128)(2,1)}), bf16[2,640,1152]{2,0,1:T(2,128)(2,1)}) %all-gather.2.cloned.1.call-update) | async-done | bytes 2949136 | tf_op jit(solution)/shard_map/all_gather | solution.py:53
  80.4 28.6 %gather_fusion = bf16[512,2,1152]{2,1,0:T(2,128)(2,1)S(1)} fusion(bf16[2,640,1152]{2,0,1:T(2,128)(2,1)} %all-gather.2.cloned.1.call-done, s32[1024]{0:T(1024)S(1)} %pad_clamp_fusion.1), kind=kCustom, calls=%fused_computation | custom fusion | bytes 4720640 | tf_op jit(solution)/shard_map/vmap(jit(_take))/gather | solution.py:56
  108.9 3.7 fusion.40
  112.7 1.6 fusion.58
  114.3 1.3 copy.114
  115.6 1.5 copy.113
  117.2 6.4 %fusion.23 = bf16[4,1,512,512]{2,3,1,0:T(8,128)(2,1)} fusion(f32[4,1,512,512]{2,3,0,1:T(8,128)} %copy.123, f32[4,1,512,512]{2,3,0,1:T(8,128)} %copy.122, f32[512,512]{0,1:T(8,128)S(1)} %bitcast.213, f32[512,512]{0,1:T(8,128)S(1)} %bitcast.216), kind=kLoop, calls=%fused_computation.42 | loop fusion | flops 4194304 | bytes 12582912 | tf_op jit(solution)/shard_map/convert.1
  123.6 2.8 fusion.31
  126.4 15.1 %fusion.27 = f32[1,4,2,512,512]{3,4,1,2,0:T(8,128)} fusion(bf16[1,2,512,512]{3,2,1,0:T(8,128)(2,1)S(1)} %copy-done.3, bf16[1,2,512,512]{3,2,1,0:T(8,128)(2,1)} %get-tuple-element.158, bf16[4,1,512,512]{2,3,1,0:T(8,128)(2,1)} %fusion.23, bf16[4,1,512,512]{2,3,1,0:T(8,128)(2,1)} %fusion.31), kind=kOutput, calls=%fused_computation.44 | convolution fusion | flops 8608808960 | bytes 14680064 | tf_op jit(solution)/shard_map/pmiax,oixy->pmoay/dot_general | solution.py:24
  141.5 6.1 %fusion.12 = f32[512,512]{0,1:T(8,128)} fusion(f32[1,4,2,512,512]{3,4,1,2,0:T(8,128)} %fusion.27), kind=kLoop, calls=%fused_computation.20 | loop fusion | flops 3932160 | bytes 9437184 | tf_op jit(solution)/shard_map/reduce_sum | solution.py:71
  147.7 1.6 copy.85
  149.3 17.2 %all-reduce.8.cloned.1.call-done = f32[1,512,512]{1,2,0:T(8,128)} async-done(((f32[1,512,512]{1,2,0:T(8,128)}), f32[1,512,512]{1,2,0:T(8,128)}) %all-reduce.8.cloned.1.call-update) | async-done | bytes 1048592 | tf_op jit(solution)/shard_map/psum | solution.py:74
  166.5 2.5 subtract_bitcast_fusion
  168.9 15.9 %fusion.24 = f32[1,4,2,512,512]{3,4,1,2,0:T(8,128)} fusion(bf16[1,2,512,512]{3,2,1,0:T(8,128)(2,1)} %get-tuple-element.159, bf16[1,2,512,512]{3,2,1,0:T(8,128)(2,1)} %get-tuple-element.156, f32[1,4,2,512,512]{3,4,1,2,0:T(8,128)} %fusion.27, f32[512,512]{0,1:T(8,128)} %subtract_bitcast_fusion), kind=kOutput, calls=%fused_computation.43 | convolution fusion | flops 8602517504 | bytes 19922944 | tf_op jit(solution)/shard_map/pmiax,oixy->pmoay/dot_general | solution.py:24
  184.8 8.1 %fusion.17 = (f32[512,512]{0,1:T(8,128)S(1)}, f32[512,512]{0,1:T(8,128)}) fusion(f32[4,1,512,512]{2,3,0,1:T(8,128)} %copy.123, f32[4,1,512,512]{2,3,0,1:T(8,128)} %copy.122, f32[1,4,2,512,512]{3,4,1,2,0:T(8,128)} %fusion.24), kind=kLoop, calls=%fused_computation.33 | loop fusion | flops 7864320 | bytes 18874368 | tf_op jit(solution)/shard_map/reduce_sum | solution.py:80
  192.9 3.6 copy.120
  196.5 1.9 copy.119
  198.5 4.8 pad_maximum_fusion.3
  203.5 4.8 fusion.3
  208.3 4.7 pad_maximum_fusion
  214.4 2.7 and_reduce_fusion
  217.1 8.7 %all-reduce.10.cloned.1.call-done = f32[1,2,512,512]{3,1,2,0:T(2,128)} async-done(((f32[1,2,512,512]{3,1,2,0:T(2,128)}), f32[1,2,512,512]{3,1,2,0:T(2,128)}) %all-reduce.10.cloned.1.call-update) | async-done | bytes 2097168 | tf_op jit(solution)/shard_map/psum | solution.py:86
  226.5 3.9 bitcast_dynamic-update-slice_fusion
  230.5 5.5 gather_fusion.1
  236.0 5.3 fusion.30
  241.3 6.8 %all-to-all-start = ((f32[1,2,640,512]{3,1,0,2:T(2,128)}), f32[1,2,640,512]{3,1,0,2:T(2,128)S(1)}, u32[]{:S(2)}, u32[]{:S(2)}) async-start(f32[1,2,640,512]{3,1,0,2:T(2,128)} %fusion.30), calls=%async_computation | async-start | bytes 5242880 | tf_op jit(solution)/shard_map/all_to_all | solution.py:94
  248.1 89.7 %all-to-all-done = f32[1,2,640,512]{3,1,0,2:T(2,128)S(1)} async-done(((f32[1,2,640,512]{3,1,0,2:T(2,128)}), f32[1,2,640,512]{3,1,0,2:T(2,128)S(1)}, u32[]{:S(2)}, u32[]{:S(2)}) %all-to-all-start) | async-done | bytes 2621472 | tf_op jit(solution)/shard_map/all_to_all | solution.py:94
  337.8 2.0 copy.92
  339.9 72.8 %while.16 = (s32[]{:T(128)}, f32[2,40,1152]{2,1,0:T(8,128)S(1)}, s32[16]{0:T(128)S(1)}, f32[16,2,40,512]{3,2,0,1:T(8,128)}, s32[]{:T(128)}, /*index=5*/s32[]{:T(128)}, s32[]{:T(128)}) while((s32[]{:T(128)}, f32[2,40,1152]{2,1,0:T(8,128)S(1)}, s32[16]{0:T(128)S(1)}, f32[16,2,40,512]{3,2,0,1:T(8,128)}, s32[]{:T(128)}, /*index=5*/s32[]{:T(128)}, ...), condition=%wide.region_8.9_spmd, body=%wide.region_7.8_spmd.sunk | while | flops 40965 | bytes 819343 | solution.py:103
  342.4 1.0 bitcast_add_fusion.2
  346.4 1.1 bitcast_add_fusion.2
  347.5 1.1 dynamic_update_slice.8
  351.0 1.0 bitcast_add_fusion.2
  355.5 1.0 bitcast_add_fusion.2
  356.5 1.2 dynamic_update_slice.8
  360.2 1.0 bitcast_add_fusion.2
  361.2 1.1 dynamic_update_slice.8
  364.8 1.0 bitcast_add_fusion.2
  365.8 1.1 dynamic_update_slice.8
  369.4 1.0 bitcast_add_fusion.2
  370.5 1.1 dynamic_update_slice.8
  374.0 1.0 bitcast_add_fusion.2
  375.0 1.2 dynamic_update_slice.8
  378.7 1.0 bitcast_add_fusion.2
  383.2 1.0 bitcast_add_fusion.2
  387.7 1.0 bitcast_add_fusion.2
  388.7 1.2 dynamic_update_slice.8
  393.4 1.1 dynamic_update_slice.8
  396.9 1.0 bitcast_add_fusion.2
  401.3 1.0 bitcast_add_fusion.2
  402.3 1.2 dynamic_update_slice.8
  410.5 1.0 bitcast_add_fusion.2
  411.5 1.2 dynamic_update_slice.8
  412.7 133.0 %all-reduce.12.cloned.1.call-done = f32[4,2,512,512]{2,3,1,0:T(8,128)} async-done(((f32[4,2,512,512]{2,3,1,0:T(8,128)}), f32[4,2,512,512]{2,3,1,0:T(8,128)}) %all-reduce.12.cloned.1.call-update) | async-done | bytes 8388624 | tf_op jit(solution)/shard_map/psum | solution.py:85
  545.7 9.9 %copy.98 = f32[4,2,512,512]{3,2,1,0:T(8,128)} copy(f32[4,2,512,512]{2,3,1,0:T(8,128)} %all-reduce.12.cloned.1.call-done) | data formatting | bytes 16777216
  (69 shorter events, 22.2 us)
Async XLA Ops:
  7.2 73.2 %all-gather.2.cloned.1.call-start = ((), (), s32[]{:S(2)}) async-start(), calls=%async_computation.1 | async-start | bytes 3133440 | tf_op jit(solution)/shard_map/all_gather | solution.py:53
  9.1 157.4 %all-reduce.8.cloned.1.call-start = ((), (), s32[]{:S(2)}) async-start(), calls=%async_computation.2 | async-start | bytes 2097152 | tf_op jit(solution)/shard_map/psum | solution.py:74
  24.1 5.3 copy-start.6
  117.1 6.4 %copy-start = (f32[4,1,512,512]{2,3,0,1:T(8,128)S(1)}, f32[4,1,512,512]{2,3,0,1:T(8,128)}, u32[]{:S(2)}) copy-start(f32[4,1,512,512]{2,3,0,1:T(8,128)} %copy.123) | copy-start | bytes 12582916
  117.2 6.4 %copy-start.1 = (f32[4,1,512,512]{2,3,0,1:T(8,128)S(1)}, f32[4,1,512,512]{2,3,0,1:T(8,128)}, u32[]{:S(2)}) copy-start(f32[4,1,512,512]{2,3,0,1:T(8,128)} %copy.122) | copy-start | bytes 12582916
  123.6 2.8 copy-start.3
  147.6 78.2 %all-reduce.10.cloned.1.call-start = ((), (), s32[]{:S(2)}) async-start(), calls=%async_computation.3 | async-start | bytes 4194304 | tf_op jit(solution)/shard_map/psum | solution.py:86
  203.3 342.4 %all-reduce.12.cloned.1.call-start = ((), (), s32[]{:S(2)}) async-start(), calls=%async_computation.4 | async-start | bytes 16777216 | tf_op jit(solution)/shard_map/psum | solution.py:85
  213.0 0.7 copy-start.5
  213.0 1.4 copy-start.4
  241.3 96.5 %all-to-all-start = ((f32[1,2,640,512]{3,1,0,2:T(2,128)}), f32[1,2,640,512]{3,1,0,2:T(2,128)S(1)}, u32[]{:S(2)}, u32[]{:S(2)}) async-start(f32[1,2,640,512]{3,1,0,2:T(2,128)} %fusion.30), calls=%async_computation | async-start | bytes 5242880 | tf_op jit(solution)/shard_map/all_to_all | solution.py:94
  412.7 142.9 %copy-start.2 = (f32[2,40,1152]{2,1,0:T(8,128)}, f32[2,40,1152]{2,1,0:T(8,128)S(1)}, u32[]{:S(2)}) copy-start(f32[2,40,1152]{2,1,0:T(8,128)S(1)} %get-tuple-element.134) | copy-start | bytes 1105924
Sparse Core Ops, SparseCore 0:
  11.4 68.9 all-gather.1
  147.8 18.6 all-reduce.7
  203.4 22.3 all-reduce.9
  232.3 313.3 all-reduce.11
where the time goes:
time: 569 us; the launch traced here: 562 us
  waiting for transfers between devices  266 us (47%)
  local copies, waits for them, and re-layouts  108 us (19%)
  other arithmetic  87.6 us (15%)
  matrix products  31 us (5%)
  loops' own time  29.7 us (5%)
  blocking collectives  16.2 us (3%)
  between operations  16.1 us (3%)
  starting transfers between devices  7.12 us (1%)
    psum x1, waiting for transfers between devices, shards(): probe_grad = lax.psum(jnp.stack([term_re, term_im], axis=1), 'scan')  133 us
    all_to_all x1, waiting for transfers between devices, shards(): lax.all_to_all(bands, 'scan', split_axis=2, concat_axis=0, tiled=True)  89.7 us
    dot_general x2, matrix products, transform(): jnp.einsum('pmiax,oixy->pmoay', half_wave, matrix_table, preferred_elemen...  31 us
    another operation x1, loops' own time, shards(): lax.fori_loop(0, devices * pat_count, add_piece, jnp.zeros((2, strip_rows...  29.7 us
    gather x1, local copies, waits for them, and re-layouts, take_patch(): band_rows = jnp.take(gathered, rows_wanted, axis=1)  28.6 us
    unnamed x24, local copies, waits for them, and re-layouts  26.3 us
    another operation x6, other arithmetic  24.3 us
    all_gather x1, waiting for transfers between devices, shards(): gathered = lax.all_gather(object_half, 'scan', axis=1, tiled=True)  17.7 us
  transfers between devices with their start and end apart: 5, of which 5 were waited for; matrix products, arithmetic and copies ran while one was open for 20% of the time, Pallas kernels for 0%

commit v1 on v0

--- a/solution.py
+++ b/solution.py
@@ -3,6 +3,7 @@
 import jax.numpy as jnp
 from jax import lax
 from jax.sharding import PartitionSpec as P
+from jax.lax import all_to_all, psum
 
 
 def dft_table(sign_factor, probe_size):
@@ -91,7 +92,19 @@
         return jnp.take(band_rows, window_of_held, axis=1)
 
     bands = jax.vmap(band_of)(patch_grad, pos_row)
-    received = lax.all_to_all(bands, "scan", split_axis=2, concat_axis=0, tiled=True)
+
+    def place_edges(arr):
+        return jnp.concatenate(
+            all_to_all(
+                jnp.stack(jnp.split(arr, psum(1, axis_name="scan"), axis=2)),
+                axis_name="scan",
+                split_axis=0,
+                concat_axis=0,
+            ),
+            axis=0,
+        )
+
+    received = place_edges(bands)
 
     def add_piece(slot_index, strip_total):
         col_start = all_cols[slot_index]

time: 569 us -> 595 us (1.046)
  local copies, waits for them, and re-layouts: 108 us -> 136 us
  other arithmetic: 87.6 us -> 70.1 us
  waiting for transfers between devices: 266 us -> 281 us
    psum x1, waiting for transfers between devices: 133 us -> 151 us  [shards(): probe_grad = lax.psum(jnp.stack([term_re, term_im], axis=1), 'scan')]
    dynamic_slice x0 -> x16, local copies, waits for them, and re-layouts: none -> 15 us  [add_piece(): received[slot_index]]
    add x16, other arithmetic: 16.6 us -> 1.83 us  [add_piece(): current + received[slot_index]]
    all_to_all x1, waiting for transfers between devices: 89.7 us -> 76 us  [place_edges(): all_to_all(jnp.stack(jnp.split(arr, psum(1, axis_name='scan'), axis=2)),...]
    psum x1, waiting for transfers between devices: 8.7 us -> 18.9 us  [shards(): patch_grad = lax.psum(patch_grad, 'mode')]
    unnamed x24 -> x41, local copies, waits for them, and re-layouts: 26.3 us -> 36 us
  transfers between devices with their start and end apart: 5 -> 5, of which waited for: 5 -> 5; matrix products, arithmetic and copies ran while one was open for 20% -> 16% of each run, Pallas kernels for 0% -> 0%
where the time goes in v1:
time: 595 us; the launch traced here: 588 us
  waiting for transfers between devices  281 us (47%)
  local copies, waits for them, and re-layouts  136 us (23%)
  other arithmetic  70.1 us (12%)
  matrix products  31 us (5%)
  loops' own time  30.4 us (5%)
  blocking collectives  16.2 us (3%)
  between operations  16.2 us (3%)
  starting transfers between devices  7 us (1%)
    psum x1, waiting for transfers between devices, shards(): probe_grad = lax.psum(jnp.stack([term_re, term_im], axis=1), 'scan')  151 us
    all_to_all x1, waiting for transfers between devices, place_edges(): all_to_all(jnp.stack(jnp.split(arr, psum(1, axis_name='scan'), axis=2)),...  76 us
    unnamed x41, local copies, waits for them, and re-layouts  36 us
    dot_general x2, matrix products, transform(): jnp.einsum('pmiax,oixy->pmoay', half_wave, matrix_table, preferred_elemen...  31 us
    another operation x1, loops' own time, shards(): lax.fori_loop(0, devices * pat_count, add_piece, jnp.zeros((2, strip_rows...  30.4 us
    gather x1, local copies, waits for them, and re-layouts, take_patch(): band_rows = jnp.take(gathered, rows_wanted, axis=1)  28.6 us
    another operation x6, other arithmetic  24.2 us
    psum x1, waiting for transfers between devices, shards(): patch_grad = lax.psum(patch_grad, 'mode')  18.9 us
  transfers between devices with their start and end apart: 5, of which 5 were waited for; matrix products, arithmetic and copies ran while one was open for 16% of the time, Pallas kernels for 0%

profile of v1, /device:TPU:0, one launch (start us, length us, event | category | flops | bytes accessed | tf_op | source)
XLA Modules:
  0.0 587.9 jit_solution(14502161718461372007)
XLA Ops:
  7.2 1.9 copy.140
  11.1 7.8 %fusion.73 = (f32[4,1,512,512]{3,2,1,0:T(8,128)}, f32[4,1,512,512]{3,2,1,0:T(8,128)}) fusion(f32[4,2,512,512]{3,2,1,0:T(8,128)} %param.11), kind=kLoop, calls=%fused_computation.136 | loop fusion | bytes 16777216 | tf_op jit(solution)/shard_map/slice | solution.py:64
  18.9 5.3 copy.133
  24.2 5.3 copy.132
  31.5 16.2 %all-reduce.3 = (s32[16]{0:T(128)S(1)}, s32[16]{0:T(128)S(1)}) all-reduce(s32[16]{0:T(128)S(1)} %dynamic-update-slice.5, s32[16]{0:T(128)S(1)} %dynamic-update-slice.6), channel_id=1, replica_groups=mesh['scan'=16,'mode'=2] {'scan'}, use_global_device_ids=true, to_apply=%add.1 | all-reduce | flops 32 | bytes 256
  48.1 4.0 multiply_convert_fusion.3
  52.1 4.4 multiply_convert_fusion.1
  56.5 4.0 negate_convert_fusion
  60.6 2.2 fusion.43
  62.7 17.6 %all-gather.2.cloned.1.call-done = bf16[2,640,1152]{2,0,1:T(2,128)(2,1)} async-done(((bf16[2,40,1152]{2,0,1:T(2,128)(2,1)}), bf16[2,640,1152]{2,0,1:T(2,128)(2,1)}) %all-gather.2.cloned.1.call-update) | async-done | bytes 2949136 | tf_op jit(solution)/shard_map/all_gather | solution.py:54
  80.3 28.6 %gather_fusion = bf16[512,2,1152]{2,1,0:T(2,128)(2,1)S(1)} fusion(bf16[2,640,1152]{2,0,1:T(2,128)(2,1)} %all-gather.2.cloned.1.call-done, s32[1024]{0:T(1024)S(1)} %pad_clamp_fusion.1), kind=kCustom, calls=%fused_computation | custom fusion | bytes 4720640 | tf_op jit(solution)/shard_map/vmap(jit(_take))/gather | solution.py:57
  108.9 3.7 fusion.40
  112.7 1.6 fusion.74
  114.3 1.3 copy.124
  115.6 1.7 copy.123
  117.3 6.4 %fusion.24 = bf16[4,1,512,512]{2,3,1,0:T(8,128)(2,1)} fusion(f32[4,1,512,512]{2,3,0,1:T(8,128)} %copy.133, f32[4,1,512,512]{2,3,0,1:T(8,128)} %copy.132, f32[512,512]{0,1:T(8,128)S(1)} %bitcast.269, f32[512,512]{0,1:T(8,128)S(1)} %bitcast.272), kind=kLoop, calls=%fused_computation.44 | loop fusion | flops 4194304 | bytes 12582912 | tf_op jit(solution)/shard_map/convert.1
  123.8 2.8 fusion.31
  126.6 15.1 %fusion.28 = f32[1,4,2,512,512]{3,4,1,2,0:T(8,128)} fusion(bf16[1,2,512,512]{3,2,1,0:T(8,128)(2,1)S(1)} %copy-done.4, bf16[1,2,512,512]{3,2,1,0:T(8,128)(2,1)} %get-tuple-element.158, bf16[4,1,512,512]{2,3,1,0:T(8,128)(2,1)} %fusion.24, bf16[4,1,512,512]{2,3,1,0:T(8,128)(2,1)} %fusion.31), kind=kOutput, calls=%fused_computation.46 | convolution fusion | flops 8608808960 | bytes 14680064 | tf_op jit(solution)/shard_map/pmiax,oixy->pmoay/dot_general | solution.py:25
  141.7 5.8 fusion.13
  147.6 1.6 copy.97
  149.2 17.2 %all-reduce.8.cloned.1.call-done = f32[1,512,512]{1,2,0:T(8,128)} async-done(((f32[1,512,512]{1,2,0:T(8,128)}), f32[1,512,512]{1,2,0:T(8,128)}) %all-reduce.8.cloned.1.call-update) | async-done | bytes 1048592 | tf_op jit(solution)/shard_map/psum | solution.py:75
  166.4 2.4 subtract_bitcast_fusion
  168.9 15.9 %fusion.25 = f32[1,4,2,512,512]{3,4,1,2,0:T(8,128)} fusion(bf16[1,2,512,512]{3,2,1,0:T(8,128)(2,1)} %get-tuple-element.159, bf16[1,2,512,512]{3,2,1,0:T(8,128)(2,1)} %get-tuple-element.156, f32[1,4,2,512,512]{3,4,1,2,0:T(8,128)} %fusion.28, f32[512,512]{0,1:T(8,128)} %subtract_bitcast_fusion), kind=kOutput, calls=%fused_computation.45 | convolution fusion | flops 8602517504 | bytes 19922944 | tf_op jit(solution)/shard_map/pmiax,oixy->pmoay/dot_general | solution.py:25
  184.7 8.1 %fusion.18 = (f32[512,512]{0,1:T(8,128)S(1)}, f32[512,512]{0,1:T(8,128)}) fusion(f32[4,1,512,512]{2,3,0,1:T(8,128)} %copy.133, f32[4,1,512,512]{2,3,0,1:T(8,128)} %copy.132, f32[1,4,2,512,512]{3,4,1,2,0:T(8,128)} %fusion.25), kind=kLoop, calls=%fused_computation.35 | loop fusion | flops 7864320 | bytes 18874368 | tf_op jit(solution)/shard_map/reduce_sum | solution.py:81
  192.9 3.6 copy.130
  196.5 1.9 copy.129
  198.4 4.8 pad_maximum_fusion.3
  204.2 2.6 and_reduce_fusion
  206.8 18.9 %all-reduce.10.cloned.1.call-done = f32[1,2,512,512]{3,1,2,0:T(2,128)} async-done(((f32[1,2,512,512]{3,1,2,0:T(2,128)}), f32[1,2,512,512]{3,1,2,0:T(2,128)}) %all-reduce.10.cloned.1.call-update) | async-done | bytes 2097168 | tf_op jit(solution)/shard_map/psum | solution.py:87
  225.8 2.2 broadcast.463
  227.9 3.4 bitcast_dynamic-update-slice_fusion
  231.4 8.8 %gather_fusion.1 = f32[640,2,512]{2,1,0:T(2,128)} fusion(f32[2,640,512]{2,0,1:T(2,128)} %bitcast_dynamic-update-slice_fusion, s32[1024]{0:T(1024)S(1)} %pad_clamp_fusion), kind=kCustom, calls=%fused_computation.1 | custom fusion | bytes 5245440 | tf_op jit(solution)/shard_map/vmap(jit(_take))/gather | solution.py:92
  240.2 3.9 bitcast_select_fusion
  254.9 6.8 %all-to-all-start = ((f32[16,1,2,40,512]{4,2,3,1,0:T(2,128)}), f32[16,1,2,40,512]{4,2,3,1,0:T(2,128)}, u32[]{:S(2)}, u32[]{:S(2)}) async-start(f32[16,1,2,40,512]{4,2,3,1,0:T(2,128)} %fusion.52), calls=%async_computation | async-start | bytes 5242880 | tf_op jit(solution)/shard_map/all_to_all | solution.py:98
  261.7 4.8 fusion.4
  266.5 4.4 pad_maximum_fusion
  271.0 76.0 %all-to-all-done = f32[16,1,2,40,512]{4,2,3,1,0:T(2,128)} async-done(((f32[16,1,2,40,512]{4,2,3,1,0:T(2,128)}), f32[16,1,2,40,512]{4,2,3,1,0:T(2,128)}, u32[]{:S(2)}, u32[]{:S(2)}) %all-to-all-start) | async-done | bytes 2621472 | tf_op jit(solution)/shard_map/all_to_all | solution.py:98
  347.0 73.5 %while.16 = (s32[]{:T(128)}, f32[2,40,1152]{2,1,0:T(8,128)S(1)}, s32[16]{0:T(128)S(1)}, f32[16,2,40,512]{3,1,2,0:T(2,128)}, s32[]{:T(128)}, /*index=5*/s32[]{:T(128)}, s32[]{:T(128)}) while((s32[]{:T(128)}, f32[2,40,1152]{2,1,0:T(8,128)S(1)}, s32[16]{0:T(128)S(1)}, f32[16,2,40,512]{3,1,2,0:T(2,128)}, s32[]{:T(128)}, /*index=5*/s32[]{:T(128)}, ...), condition=%wide.region_8.9_spmd, body=%wide.region_7.8_spmd.sunk | while | flops 40965 | bytes 1147023 | solution.py:116
  347.0 1.0 constant_dynamic-slice_fusion.2
  351.2 0.9 constant_dynamic-slice_fusion.2
  354.7 1.1 dynamic_update_slice.8
  359.3 1.0 dynamic_update_slice.8
  360.3 0.9 constant_dynamic-slice_fusion.2
  363.9 1.2 dynamic_update_slice.8
  365.1 0.9 constant_dynamic-slice_fusion.2
  368.6 1.1 dynamic_update_slice.8
  373.2 1.1 dynamic_update_slice.8
  374.4 0.9 constant_dynamic-slice_fusion.2
  377.9 1.1 dynamic_update_slice.8
  379.0 0.9 constant_dynamic-slice_fusion.2
  382.5 1.2 dynamic_update_slice.8
  387.2 1.0 dynamic_update_slice.8
  388.3 0.9 constant_dynamic-slice_fusion.2
  391.8 1.0 dynamic_update_slice.8
  392.8 0.9 constant_dynamic-slice_fusion.2
  396.3 1.2 dynamic_update_slice.8
  397.5 0.9 constant_dynamic-slice_fusion.2
  401.1 1.1 dynamic_update_slice.8
  410.0 1.2 dynamic_update_slice.8
  411.2 0.9 constant_dynamic-slice_fusion.2
  414.8 1.0 dynamic_update_slice.8
  419.3 1.2 dynamic_update_slice.8
  420.5 150.8 %all-reduce.12.cloned.1.call-done = f32[4,2,512,512]{2,3,1,0:T(8,128)} async-done(((f32[4,2,512,512]{2,3,1,0:T(8,128)}), f32[4,2,512,512]{2,3,1,0:T(8,128)}) %all-reduce.12.cloned.1.call-update) | async-done | bytes 8388624 | tf_op jit(solution)/shard_map/psum | solution.py:86
  571.3 9.9 %copy.108 = f32[4,2,512,512]{3,2,1,0:T(8,128)} copy(f32[4,2,512,512]{2,3,1,0:T(8,128)} %all-reduce.12.cloned.1.call-done) | data formatting | bytes 16777216
  (102 shorter events, 32.9 us)
Async XLA Ops:
  7.2 73.2 %all-gather.2.cloned.1.call-start = ((), (), s32[]{:S(2)}) async-start(), calls=%async_computation.1 | async-start | bytes 3133440 | tf_op jit(solution)/shard_map/all_gather | solution.py:54
  9.1 157.3 %all-reduce.8.cloned.1.call-start = ((), (), s32[]{:S(2)}) async-start(), calls=%async_computation.2 | async-start | bytes 2097152 | tf_op jit(solution)/shard_map/psum | solution.py:75
  24.2 5.3 copy-start.7
  117.3 6.4 %copy-start = (f32[4,1,512,512]{2,3,0,1:T(8,128)S(1)}, f32[4,1,512,512]{2,3,0,1:T(8,128)}, u32[]{:S(2)}) copy-start(f32[4,1,512,512]{2,3,0,1:T(8,128)} %copy.133) | copy-start | bytes 12582916
  117.3 6.4 %copy-start.1 = (f32[4,1,512,512]{2,3,0,1:T(8,128)S(1)}, f32[4,1,512,512]{2,3,0,1:T(8,128)}, u32[]{:S(2)}) copy-start(f32[4,1,512,512]{2,3,0,1:T(8,128)} %copy.132) | copy-start | bytes 12582916
  123.8 2.8 copy-start.4
  147.6 78.2 %all-reduce.10.cloned.1.call-start = ((), (), s32[]{:S(2)}) async-start(), calls=%async_computation.3 | async-start | bytes 4194304 | tf_op jit(solution)/shard_map/psum | solution.py:87
  198.4 5.1 copy-start.6
  198.4 5.8 copy-start.5
  225.8 2.2 copy-start.3
  254.9 92.2 %all-to-all-start = ((f32[16,1,2,40,512]{4,2,3,1,0:T(2,128)}), f32[16,1,2,40,512]{4,2,3,1,0:T(2,128)}, u32[]{:S(2)}, u32[]{:S(2)}) async-start(f32[16,1,2,40,512]{4,2,3,1,0:T(2,128)} %fusion.52), calls=%async_computation | async-start | bytes 5242880 | tf_op jit(solution)/shard_map/all_to_all | solution.py:98
  261.7 309.6 %all-reduce.12.cloned.1.call-start = ((), (), s32[]{:S(2)}) async-start(), calls=%async_computation.4 | async-start | bytes 16777216 | tf_op jit(solution)/shard_map/psum | solution.py:86
  420.5 160.7 %copy-start.2 = (f32[2,40,1152]{2,1,0:T(8,128)}, f32[2,40,1152]{2,1,0:T(8,128)S(1)}, u32[]{:S(2)}) copy-start(f32[2,40,1152]{2,1,0:T(8,128)S(1)} %get-tuple-element.134) | copy-start | bytes 1105924
Sparse Core Ops, SparseCore 0:
  11.4 68.9 all-gather.1
  147.7 18.6 all-reduce.7
  203.3 22.3 all-reduce.9
  271.1 300.1 all-reduce.11
